TPU v7x, 32 devices: a whole 2x2x4 slice. The times are simulated.
32 devices in a mesh: island: 4 (over x, core), fsdp: 8 (over z, y).
Axes of the slice: x: 2, y: 2, z: 4, core: 2. Of those that a mesh axis runs over, the one named last changes fastest.
Arguments:
- pseudo_grads: bfloat16 [4, 8192, 1024], P('island', 'fsdp'), as said below
- outer_params: float32 [8192, 1024], P('fsdp'), may hold values from -3 to 3
- momentum: float32 [8192, 1024], P('fsdp'), may hold values from -6 to 6
Outputs:
- new_params: float32 [8192, 1024], P('fsdp')
- new_momentum: float32 [8192, 1024], P('fsdp')
Inputs may be any that keep to these rules, and one draw needn't show every extreme that they name: `pseudo_grads`: finite bfloat16 values.
All inputs are finite; a program needn't handle non-finite values.
Results may differ from a plain program's by a relative error of at most 0.0003.
Values sent between devices are 32-bit elements; how exact they have to be, the bound alone decides.
A program may use at most 64 MiB of HBM per device.

v0:
```python
import math

import jax
import jax.numpy as jnp
from jax import lax
from jax.sharding import PartitionSpec as P

D = 8192
KV = 1024


def outer_update(average, squares, outer_rows, moment_rows):
    threshold = 0.2 * math.sqrt(D * KV)
    factor = jnp.minimum(1.0, threshold / jnp.sqrt(squares + 1e-06))
    clipped = factor * average
    moment_next = 0.9 * moment_rows + clipped
    params_next = outer_rows - 0.7 * (clipped + 0.9 * moment_next)
    return (params_next, moment_next)


def per_device(pseudo_grads, outer_params, momentum):
    local_term = pseudo_grads[0].astype(jnp.float32)
    replicas = lax.axis_size("island")
    total = lax.psum(local_term, "island")
    average = total / replicas
    squares = lax.psum(jnp.sum(average * average), "fsdp")
    return outer_update(average, squares, outer_params, momentum)


def solution(mesh):
    return jax.shard_map(
        per_device,
        mesh=mesh,
        in_specs=(P("island", "fsdp", None), P("fsdp", None), P("fsdp", None)),
        out_specs=(P("fsdp", None), P("fsdp", None)),
        check_vma=False,
    )
```

profile of v0, /device:TPU:0, one launch (start us, length us, event | category | flops | bytes accessed | tf_op | source)
XLA Modules:
  0.0 143.7 jit_solution(15854074300530472107)
XLA Ops:
  7.2 0.0 all-reduce.2.cloned.1.call-start
  7.2 4.1 %bitcast_convert_fusion = f32[1024,1024]{1,0:T(8,128)} fusion(bf16[1,1024,1024]{2,1,0:T(8,128)(2,1)} %param.3), kind=kLoop, calls=%fused_computation.3 | loop fusion | flops 1048576 | bytes 6291456 | tf_op jit(solution)/shard_map/convert_element_type | solution.py:22
  11.3 0.0 all-reduce.2.cloned.1.call-update
  11.3 88.3 %all-reduce.2.cloned.1.call-done = f32[1024,1024]{1,0:T(8,128)} async-done(((f32[1024,1024]{1,0:T(8,128)}), f32[1024,1024]{1,0:T(8,128)}) %all-reduce.2.cloned.1.call-update) | async-done | bytes 4194320 | tf_op jit(solution)/shard_map/psum | solution.py:24
  99.6 3.9 %multiply_reduce_fusion = f32[]{:T(128)} fusion(f32[1024,1024]{1,0:T(8,128)} %all-reduce.2.cloned.1.call-done), kind=kLoop, calls=%fused_computation.2 | loop fusion | flops 3145727 | bytes 4194308 | tf_op jit(solution)/shard_map/reduce_sum | solution.py:26
  103.5 22.0 %psum.15 = f32[]{:T(128)} all-reduce(f32[]{:T(128)} %multiply_reduce_fusion), channel_id=1, replica_groups=mesh['island'=4,'fsdp'=8] {'fsdp'}, use_global_device_ids=true, to_apply=%region_2.0 | all-reduce | flops 1 | bytes 8 | tf_op jit(solution)/shard_map/psum | solution.py:26
  126.2 10.6 %multiply_subtract_fusion = (f32[1024,1024]{1,0:T(8,128)}, f32[1024,1024]{1,0:T(8,128)}) fusion(f32[1024,1024]{1,0:T(8,128)} %param.4, f32[1024,1024]{1,0:T(8,128)} %all-reduce.2.cloned.1.call-done, f32[]{:T(128)S(6)} %mul.24, f32[1024,1024]{1,0:T(8,128)} %param.5), kind=kLoop, calls=%fused_computation | loop fusion | flops 7340032 | bytes 20971524 | tf_op jit(solution)/shard_map/sub | solution.py:17
Async XLA Ops:
  7.2 92.5 %all-reduce.2.cloned.1.call-start = ((), (), s32[]{:S(2)}) async-start(), calls=%async_computation | async-start | bytes 8388608 | tf_op jit(solution)/shard_map/psum | solution.py:24
Sparse Core Ops, SparseCore 0:
  11.4 88.1 all-reduce.1
where the time goes:
time: 144 us
  waiting for transfers between devices  88.3 us (61%)
  blocking collectives  22 us (15%)
  other arithmetic  18.6 us (13%)
  between operations  14.7 us (10%)
    psum x1, waiting for transfers between devices, per_device(): total = lax.psum(local_term, 'island')  88.3 us
    psum x1, blocking collectives, per_device(): squares = lax.psum(jnp.sum(average * average), 'fsdp')  22 us
    sub x1, other arithmetic, outer_update(): params_next = outer_rows - 0.7 * (clipped + 0.9 * moment_next)  10.6 us
    convert_element_type x1, other arithmetic, per_device(): local_term = pseudo_grads[0].astype(jnp.float32)  4.07 us
    reduce_sum x1, other arithmetic, per_device(): squares = lax.psum(jnp.sum(average * average), 'fsdp')  3.87 us
  transfers between devices with their start and end apart: 1, of which 1 were waited for; matrix products, arithmetic and copies ran while one was open for 0% of the time, Pallas kernels for 0%

commit v1 on v0

v1 whole, which is shorter than its diff:
```python
import functools
import math

import jax
import jax.numpy as jnp
from jax import lax
from jax.experimental import pallas as pl
from jax.experimental.pallas import tpu as pltpu
from jax.sharding import PartitionSpec as P

MESH = pl.DeviceIdType.MESH
CORES = 2


def fold(block):
    total = None
    for r in range(0, block.shape[0], 8):
        for c in range(0, block.shape[1], 128):
            tile = block[r : r + 8, c : c + 128]
            total = tile if total is None else total + tile
    return total


def kernel(
    chips, groups, chunk, grads, average, squares,
    local, staged, paired, outgoing, arrived, pair_sums, chip_sums, group_sums,
    load_sem, pair_send, pair_recv, part_send, part_recv, full_send, full_recv,
    share_send, share_recv, sum_send, sum_recv,
):
    rows, cols = average.shape
    half = rows // CORES
    piece = half // chips
    count = piece // chunk
    island = lax.axis_index("island")
    group = lax.axis_index("fsdp")
    chip, core = lax.div(island, CORES), lax.rem(island, CORES)
    other = 1 - core
    sibling = {"island": chip * CORES + other}

    def owner(p):
        return lax.rem(chip + p, chips)

    def peer(p):
        return {"island": owner(p) * CORES + core}

    def start_of(which_core, p, j):
        return pl.multiple_of(which_core * half + owner(p) * piece + j * chunk, chunk)

    def span(j):
        return pl.ds(pl.multiple_of(j * chunk, chunk), chunk)

    barrier = pltpu.get_barrier_semaphore()
    pl.semaphore_signal(barrier, inc=1, device_id=sibling, device_id_type=MESH)
    for p in range(1, chips):
        pl.semaphore_signal(barrier, inc=1, device_id=peer(p), device_id_type=MESH)
    for s in range(1, groups):
        pl.semaphore_signal(
            barrier, inc=1, device_id={"fsdp": lax.rem(group + s, groups)}, device_id_type=MESH
        )

    def load(side, p):
        which = other if side == 0 else core
        place = pl.ds(start_of(which, p, 0), piece)
        return pltpu.make_async_copy(
            grads.at[0, place], local.at[place], load_sem.at[side, p]
        )

    order = [*range(1, chips), 0]
    for p in order:
        load(0, p).start()
        load(1, p).start()

    def to_sibling(p, j):
        return pltpu.make_async_remote_copy(
            staged.at[p, span(j)], paired.at[p, span(j)],
            pair_send.at[p, j], pair_recv.at[p, j], sibling, MESH,
        )

    def part_to_peer(p, j, back):
        slot = (chips - p if back else p) - 1
        return pltpu.make_async_remote_copy(
            outgoing.at[p - 1, span(j)], arrived.at[slot, span(j)],
            part_send.at[p - 1, j], part_recv.at[slot, j], peer(p), MESH,
        )

    def full_to_peer(p, j, whose, slot):
        place = pl.ds(start_of(core, whose, j), chunk)
        return pltpu.make_async_remote_copy(
            average.at[place], average.at[place],
            full_send.at[p - 1, j], full_recv.at[slot - 1, j], peer(p), MESH,
        )

    def full_to_sibling(p, j, which):
        place = pl.ds(start_of(which, p, j), chunk)
        return pltpu.make_async_remote_copy(
            average.at[place], average.at[place],
            share_send.at[p, j], share_recv.at[p, j], sibling, MESH,
        )

    def each(body):
        lax.fori_loop(0, count, lambda j, _: body(j), None)

    def send_pair(p):
        load(0, p).wait()

        def body(j):
            block = local[pl.ds(start_of(other, p, j), chunk)]
            staged[p, span(j)] = block.astype(jnp.float32)
            to_sibling(p, j).start()

        each(body)

    def chip_sum(p, j):
        to_sibling(p, j).wait_recv()
        mine = local[pl.ds(start_of(core, p, j), chunk)].astype(jnp.float32)
        return mine + paired[p, span(j)]

    pl.semaphore_wait(barrier, 1 + (chips - 1) + (groups - 1))
    for p in range(1, chips):
        send_pair(p)
    for p in range(1, chips):
        load(1, p).wait()

        def send_part(j, p=p):
            outgoing[p - 1, span(j)] = chip_sum(p, j)
            part_to_peer(p, j, True).start()

        each(send_part)
    send_pair(0)
    load(1, 0).wait()

    def finish(j, partial):
        total = chip_sum(0, j)
        for p in range(1, chips):
            part_to_peer(p, j, False).wait_recv()
            total = total + arrived[p - 1, span(j)]
        mean = total / (chips * CORES)
        average[pl.ds(start_of(core, 0, j), chunk)] = mean
        for p in range(1, chips):
            full_to_peer(p, j, 0, chips - p).start()
        full_to_sibling(0, j, core).start()
        return partial + fold(mean * mean)

    partial = lax.fori_loop(0, count, finish, jnp.zeros((8, 128), jnp.float32))

    def exchange(slots, mine, value, targets, first):
        slots[mine] = value
        copies = []
        for s, target in enumerate(targets):
            copy = pltpu.make_async_remote_copy(
                slots.at[mine], slots.at[mine],
                sum_send.at[first + s], sum_recv.at[first + s], target, MESH,
            )
            copy.start()
            copies.append(copy)
        for copy in copies:
            copy.wait_recv()
        total = slots[0]
        for s in range(1, slots.shape[0]):
            total = total + slots[s]
        return total, copies

    total, sent_a = exchange(pair_sums, core, partial, [sibling], 0)
    total, sent_b = exchange(chip_sums, chip, total, [peer(p) for p in range(1, chips)], 1)
    total, sent_c = exchange(
        group_sums, group, total,
        [{"fsdp": lax.rem(group + s, groups)} for s in range(1, groups)], chips,
    )
    squares[...] = jnp.broadcast_to(jnp.sum(total), squares.shape)

    def forward(j):
        for p in range(1, chips):
            full_to_peer(p, j, p, p).wait_recv()
            full_to_sibling(p, j, core).start()

    each(forward)

    def close(j):
        for p in range(chips):
            full_to_sibling(p, j, other).wait_recv()
            full_to_sibling(p, j, core).wait_send()
            to_sibling(p, j).wait_send()
        for p in range(1, chips):
            part_to_peer(p, j, True).wait_send()
            full_to_peer(p, j, 0, p).wait_send()

    each(close)
    for copy in sent_a + sent_b + sent_c:
        copy.wait_send()


def mean_and_squares(grads, islands, groups):
    rows, cols = grads.shape[1:]
    chips = islands // CORES
    piece = rows // islands
    chunk = max(16, piece // 8)
    count = piece // chunk
    wide = jnp.float32
    dma = pltpu.SemaphoreType.DMA
    return pl.pallas_call(
        functools.partial(kernel, chips, groups, chunk),
        out_shape=[
            jax.ShapeDtypeStruct((rows, cols), wide),
            jax.ShapeDtypeStruct((8, 128), wide),
        ],
        in_specs=[pl.BlockSpec(memory_space=pl.ANY)],
        out_specs=[pl.BlockSpec(memory_space=pltpu.VMEM)] * 2,
        scratch_shapes=[
            pltpu.VMEM((rows, cols), grads.dtype),
            pltpu.VMEM((chips, piece, cols), wide),
            pltpu.VMEM((chips, piece, cols), wide),
            pltpu.VMEM((max(chips - 1, 1), piece, cols), wide),
            pltpu.VMEM((max(chips - 1, 1), piece, cols), wide),
            pltpu.VMEM((CORES, 8, 128), wide),
            pltpu.VMEM((chips, 8, 128), wide),
            pltpu.VMEM((groups, 8, 128), wide),
            dma((2, chips)),
            dma((chips, count)),
            dma((chips, count)),
            dma((chips - 1, count)),
            dma((chips - 1, count)),
            dma((chips - 1, count)),
            dma((chips - 1, count)),
            dma((chips, count)),
            dma((chips, count)),
            dma((chips + groups - 1,)),
            dma((chips + groups - 1,)),
        ],
        compiler_params=pltpu.CompilerParams(
            collective_id=0, has_side_effects=True, vmem_limit_bytes=24 * 2**20
        ),
        cost_estimate=pl.CostEstimate(
            flops=8 * rows * cols, bytes_accessed=6 * rows * cols, transcendentals=0
        ),
    )(grads)


def per_device(pseudo_grads, outer_params, momentum):
    rows, cols = outer_params.shape
    groups = lax.axis_size("fsdp")
    average, sums = mean_and_squares(pseudo_grads, lax.axis_size("island"), groups)
    squares = sums[0, 0]
    threshold = 0.2 * math.sqrt(rows * groups * cols)
    factor = jnp.minimum(1.0, threshold / jnp.sqrt(squares + 1e-06))
    clipped = factor * average
    moment_next = 0.9 * momentum + clipped
    params_next = outer_params - 0.7 * (clipped + 0.9 * moment_next)
    return params_next, moment_next


def solution(mesh):
    return jax.shard_map(
        per_device,
        mesh=mesh,
        in_specs=(P("island", "fsdp", None), P("fsdp", None), P("fsdp", None)),
        out_specs=(P("fsdp", None), P("fsdp", None)),
        check_vma=False,
    )
```

time: 144 us -> 72.9 us (0.51)
  waiting for transfers between devices: 88.3 us -> 0 us
  Pallas kernels: 0 us -> 60.4 us
  blocking collectives: 22 us -> 0 us
  between operations: 14.7 us -> 1.34 us
  other arithmetic: 18.6 us -> 8.93 us
  local copies, waits for them, and re-layouts: 0 us -> 2.1 us
    psum x1 -> x0, waiting for transfers between devices: 88.3 us -> none  [per_device(): total = lax.psum(local_term, 'island')]
    pallas_call x0 -> x1, Pallas kernels: none -> 60.4 us  [mean_and_squares(): pl.pallas_call(functools.partial(kernel, chips, groups, chunk), out_shape...]
    psum x1 -> x0, blocking collectives: 22 us -> none  [per_device(): squares = lax.psum(jnp.sum(average * average), 'fsdp')]
    convert_element_type x1 -> x0, other arithmetic: 4.07 us -> none  [per_device(): local_term = pseudo_grads[0].astype(jnp.float32)]
    reduce_sum x1 -> x0, other arithmetic: 3.87 us -> none  [per_device(): squares = lax.psum(jnp.sum(average * average), 'fsdp')]
    sub x1, other arithmetic: 10.6 us -> 8.93 us  [per_device(): params_next = outer_params - 0.7 * (clipped + 0.9 * moment_next)]
    unnamed x0 -> x2, local copies, waits for them, and re-layouts: none -> 1.58 us
  transfers between devices with their start and end apart: 1 -> 0, of which waited for: 1 -> 0; matrix products, arithmetic and copies ran while one was open for 0% -> 0% of each run, Pallas kernels for 0% -> 0%
where the time goes in v1:
time: 72.9 us; the launch traced here: 72.7 us
  Pallas kernels  60.4 us (83%)
  other arithmetic  8.93 us (12%)
  local copies, waits for them, and re-layouts  2.1 us (3%)
  between operations  1.34 us (2%)
    pallas_call x1, Pallas kernels, mean_and_squares(): pl.pallas_call(functools.partial(kernel, chips, groups, chunk), out_shape...  60.4 us
    sub x1, other arithmetic, per_device(): params_next = outer_params - 0.7 * (clipped + 0.9 * moment_next)  8.93 us
    unnamed x2, local copies, waits for them, and re-layouts  1.58 us

profile of v1, /device:TPU:0, one launch (start us, length us, event | category | flops | bytes accessed | tf_op | source)
XLA Modules:
  0.0 72.7 jit_solution(18168254412993109252)
XLA Ops:
  0.6 0.0 copy-start
  0.6 1.6 %copy-done = bf16[1,1024,1024]{2,1,0:T(8,128)(2,1)S(1)} copy-done((bf16[1,1024,1024]{2,1,0:T(8,128)(2,1)S(1)}, bf16[1,1024,1024]{2,1,0:T(8,128)(2,1)}, u32[]{:S(2)}) %copy-start) | copy-done | bytes 2097176
  2.2 60.4 %shard_map.50 = (f32[1024,1024]{1,0:T(8,128)S(1)}, f32[8,128]{1,0:T(8,128)S(1)}) custom-call(bf16[1,1024,1024]{2,1,0:T(8,128)(2,1)S(1)} %copy-done), custom_call_target="tpu_custom_call" | custom-call | flops 8388608 | bytes 6291456 | tf_op jit(solution)/shard_map/pallas_call | solution.py:200
  62.6 0.5 slice.3
  63.8 8.9 %multiply_subtract_fusion = (f32[1024,1024]{1,0:T(8,128)}, f32[1024,1024]{1,0:T(8,128)}) fusion(f32[1024,1024]{1,0:T(8,128)} %param.4, f32[1024,1024]{1,0:T(8,128)S(1)} %get-tuple-element.5, f32[]{:T(128)} %bitcast, f32[1024,1024]{1,0:T(8,128)} %param.5), kind=kLoop, calls=%fused_computation | loop fusion | flops 7340032 | bytes 20971524 | tf_op jit(solution)/shard_map/sub | solution.py:247
Async XLA Ops:
  0.6 1.6 %copy-start = (bf16[1,1024,1024]{2,1,0:T(8,128)(2,1)S(1)}, bf16[1,1024,1024]{2,1,0:T(8,128)(2,1)}, u32[]{:S(2)}) copy-start(bf16[1,1024,1024]{2,1,0:T(8,128)(2,1)} %grads.1) | copy-start | bytes 6291460

commit v2 on v1

--- a/solution.py
+++ b/solution.py
@@ -10,6 +10,8 @@
 
 MESH = pl.DeviceIdType.MESH
 CORES = 2
+CHUNKS = 8
+AHEAD = 2
 
 
 def fold(block):
@@ -22,9 +24,9 @@
 
 
 def kernel(
-    chips, groups, chunk, grads, average, squares,
-    local, staged, paired, outgoing, arrived, pair_sums, chip_sums, group_sums,
-    load_sem, pair_send, pair_recv, part_send, part_recv, full_send, full_recv,
+    chips, groups, chunk, threshold, grads, outer, moment, params_out, moment_out,
+    average, local, staged, paired, outgoing, arrived, pair_sums, chip_sums, group_sums,
+    load_sem, state_sem, pair_send, pair_recv, part_send, part_recv, full_send, full_recv,
     share_send, share_recv, sum_send, sum_recv,
 ):
     rows, cols = average.shape
@@ -70,6 +72,11 @@
         load(0, p).start()
         load(1, p).start()
 
+    state = [
+        pltpu.make_async_copy(outer, params_out, state_sem.at[0]),
+        pltpu.make_async_copy(moment, moment_out, state_sem.at[1]),
+    ]
+
     def to_sibling(p, j):
         return pltpu.make_async_remote_copy(
             staged.at[p, span(j)], paired.at[p, span(j)],
@@ -128,6 +135,12 @@
         each(send_part)
     send_pair(0)
     load(1, 0).wait()
+    for copy in state:
+        copy.start()
+
+    def gather(j):
+        for p in range(1, chips):
+            full_to_peer(p, j, 0, chips - p).start()
 
     def finish(j, partial):
         total = chip_sum(0, j)
@@ -136,14 +149,13 @@
             total = total + arrived[p - 1, span(j)]
         mean = total / (chips * CORES)
         average[pl.ds(start_of(core, 0, j), chunk)] = mean
-        for p in range(1, chips):
-            full_to_peer(p, j, 0, chips - p).start()
+        pl.when(j < AHEAD)(lambda: gather(j))
         full_to_sibling(0, j, core).start()
         return partial + fold(mean * mean)
 
     partial = lax.fori_loop(0, count, finish, jnp.zeros((8, 128), jnp.float32))
 
-    def exchange(slots, mine, value, targets, first):
+    def send_sum(slots, mine, value, targets, first):
         slots[mine] = value
         copies = []
         for s, target in enumerate(targets):
@@ -153,31 +165,66 @@
             )
             copy.start()
             copies.append(copy)
+        return copies
+
+    def take_sum(slots, copies):
         for copy in copies:
             copy.wait_recv()
         total = slots[0]
         for s in range(1, slots.shape[0]):
             total = total + slots[s]
-        return total, copies
-
-    total, sent_a = exchange(pair_sums, core, partial, [sibling], 0)
-    total, sent_b = exchange(chip_sums, chip, total, [peer(p) for p in range(1, chips)], 1)
-    total, sent_c = exchange(
+        return total
+
+    sent_a = send_sum(chip_sums, chip, partial, [peer(p) for p in range(1, chips)], 1)
+
+    def gather_rest(j, _):
+        gather(j)
+
+    lax.fori_loop(min(AHEAD, count), count, gather_rest, None)
+    total = take_sum(chip_sums, sent_a)
+    sent_b = send_sum(pair_sums, core, total, [sibling], 0)
+    total = take_sum(pair_sums, sent_b)
+    sent_c = send_sum(
         group_sums, group, total,
         [{"fsdp": lax.rem(group + s, groups)} for s in range(1, groups)], chips,
     )
-    squares[...] = jnp.broadcast_to(jnp.sum(total), squares.shape)
+    squares = jnp.sum(take_sum(group_sums, sent_c), keepdims=True)
+    factor = jnp.minimum(1.0, threshold / jnp.sqrt(squares + 1e-06))
+    for copy in state:
+        copy.wait()
+
+    def update(which, p, j):
+        place = pl.ds(start_of(which, p, j), chunk)
+        clipped = factor * average[place]
+        moment_next = 0.9 * moment_out[place] + clipped
+        moment_out[place] = moment_next
+        params_out[place] = params_out[place] - 0.7 * (clipped + 0.9 * moment_next)
+
+    def own(j):
+        update(core, 0, j)
+        full_to_sibling(0, j, other).wait_recv()
+        update(other, 0, j)
+
+    each(own)
+
+    def from_sibling(j):
+        for p in range(1, chips):
+            full_to_sibling(p, j, other).wait_recv()
+            update(other, p, j)
 
     def forward(j):
         for p in range(1, chips):
             full_to_peer(p, j, p, p).wait_recv()
             full_to_sibling(p, j, core).start()
+        for p in range(1, chips):
+            update(core, p, j)
+        pl.when(j > 0)(lambda: from_sibling(j - 1))
 
     each(forward)
+    from_sibling(count - 1)
 
     def close(j):
         for p in range(chips):
-            full_to_sibling(p, j, other).wait_recv()
             full_to_sibling(p, j, core).wait_send()
             to_sibling(p, j).wait_send()
         for p in range(1, chips):
@@ -189,23 +236,22 @@
         copy.wait_send()
 
 
-def mean_and_squares(grads, islands, groups):
-    rows, cols = grads.shape[1:]
+def step(islands, groups, grads, outer, moment):
+    rows, cols = outer.shape
     chips = islands // CORES
     piece = rows // islands
-    chunk = max(16, piece // 8)
+    chunk = max(16, piece // CHUNKS)
     count = piece // chunk
+    threshold = 0.2 * math.sqrt(rows * groups * cols)
     wide = jnp.float32
     dma = pltpu.SemaphoreType.DMA
     return pl.pallas_call(
-        functools.partial(kernel, chips, groups, chunk),
-        out_shape=[
-            jax.ShapeDtypeStruct((rows, cols), wide),
-            jax.ShapeDtypeStruct((8, 128), wide),
-        ],
-        in_specs=[pl.BlockSpec(memory_space=pl.ANY)],
+        functools.partial(kernel, chips, groups, chunk, threshold),
+        out_shape=[pltpu.VMEM((rows, cols), wide)] * 2,
+        in_specs=[pl.BlockSpec(memory_space=pltpu.HBM)] * 3,
         out_specs=[pl.BlockSpec(memory_space=pltpu.VMEM)] * 2,
         scratch_shapes=[
+            pltpu.VMEM((rows, cols), wide),
             pltpu.VMEM((rows, cols), grads.dtype),
             pltpu.VMEM((chips, piece, cols), wide),
             pltpu.VMEM((chips, piece, cols), wide),
@@ -215,6 +261,7 @@
             pltpu.VMEM((chips, 8, 128), wide),
             pltpu.VMEM((groups, 8, 128), wide),
             dma((2, chips)),
+            dma((2,)),
             dma((chips, count)),
             dma((chips, count)),
             dma((chips - 1, count)),
@@ -227,25 +274,17 @@
             dma((chips + groups - 1,)),
         ],
         compiler_params=pltpu.CompilerParams(
-            collective_id=0, has_side_effects=True, vmem_limit_bytes=24 * 2**20
+            collective_id=0, has_side_effects=True, vmem_limit_bytes=32 * 2**20
         ),
         cost_estimate=pl.CostEstimate(
-            flops=8 * rows * cols, bytes_accessed=6 * rows * cols, transcendentals=0
+            flops=16 * rows * cols, bytes_accessed=10 * rows * cols, transcendentals=0
         ),
-    )(grads)
+    )(*(pltpu.with_memory_space_constraint(x, pltpu.HBM) for x in (grads, outer, moment)))
 
 
 def per_device(pseudo_grads, outer_params, momentum):
-    rows, cols = outer_params.shape
-    groups = lax.axis_size("fsdp")
-    average, sums = mean_and_squares(pseudo_grads, lax.axis_size("island"), groups)
-    squares = sums[0, 0]
-    threshold = 0.2 * math.sqrt(rows * groups * cols)
-    factor = jnp.minimum(1.0, threshold / jnp.sqrt(squares + 1e-06))
-    clipped = factor * average
-    moment_next = 0.9 * momentum + clipped
-    params_next = outer_params - 0.7 * (clipped + 0.9 * moment_next)
-    return params_next, moment_next
+    islands, groups = lax.axis_size("island"), lax.axis_size("fsdp")
+    return tuple(step(islands, groups, pseudo_grads, outer_params, momentum))
 
 
 def solution(mesh):

time: 72.9 us -> 61.2 us (0.84)
  other arithmetic: 8.93 us -> 0 us
  Pallas kernels: 60.4 us -> 56.4 us
  local copies, waits for them, and re-layouts: 2.1 us -> 4.03 us
    sub x1 -> x0, other arithmetic: 8.93 us -> none  [per_device(): params_next = outer_params - 0.7 * (clipped + 0.9 * moment_next)]
    pallas_call x1, Pallas kernels: 60.4 us -> 56.4 us  [step(): pl.pallas_call(functools.partial(kernel, chips, groups, chunk, threshold)...]
    unnamed x2, local copies, waits for them, and re-layouts: 1.58 us -> 4.03 us
where the time goes in v2:
time: 61.2 us; the launch traced here: 61.1 us
  Pallas kernels  56.4 us (92%)
  local copies, waits for them, and re-layouts  4.03 us (7%)
  between operations  0.64 us (1%)
    pallas_call x1, Pallas kernels, step(): pl.pallas_call(functools.partial(kernel, chips, groups, chunk, threshold)...  56.4 us
    unnamed x2, local copies, waits for them, and re-layouts  4.03 us

profile of v2, /device:TPU:0, one launch (start us, length us, event | category | flops | bytes accessed | tf_op | source)
XLA Modules:
  0.0 61.1 jit_solution(14319575135477314687)
XLA Ops:
  0.6 56.4 %shard_map.50 = (f32[1024,1024]{1,0:T(8,128)S(1)}, f32[1024,1024]{1,0:T(8,128)S(1)}) custom-call(bf16[1,1024,1024]{2,1,0:T(8,128)(2,1)} %grads.1, f32[1024,1024]{1,0:T(8,128)} %outer.1, f32[1024,1024]{1,0:T(8,128)} %moment.1), custom_call_target="tpu_custom_call" | custom-call | flops 16777216 | bytes 10485760 | tf_op jit(solution)/shard_map/pallas_call | solution.py:248
  57.1 2.0 %copy.7 = f32[1024,1024]{1,0:T(8,128)} copy(f32[1024,1024]{1,0:T(8,128)S(1)} %get-tuple-element.2) | data formatting | bytes 8388608
  59.1 2.0 %copy.8 = f32[1024,1024]{1,0:T(8,128)} copy(f32[1024,1024]{1,0:T(8,128)S(1)} %get-tuple-element.3) | data formatting | bytes 8388608

commit v3 on v2

--- a/solution.py
+++ b/solution.py
@@ -12,6 +12,7 @@
 CORES = 2
 CHUNKS = 8
 AHEAD = 2
+STORES = 4
 
 
 def fold(block):
@@ -25,9 +26,9 @@
 
 def kernel(
     chips, groups, chunk, threshold, grads, outer, moment, params_out, moment_out,
-    average, local, staged, paired, outgoing, arrived, pair_sums, chip_sums, group_sums,
+    average, local, staged, paired, outgoing, arrived, pair_sums, chip_sums, group_sums, total_sum,
     load_sem, state_sem, pair_send, pair_recv, part_send, part_recv, full_send, full_recv,
-    share_send, share_recv, sum_send, sum_recv,
+    share_send, share_recv, sum_send, sum_recv, ready,
 ):
     rows, cols = average.shape
     half = rows // CORES
@@ -52,13 +53,22 @@
         return pl.ds(pl.multiple_of(j * chunk, chunk), chunk)
 
     barrier = pltpu.get_barrier_semaphore()
-    pl.semaphore_signal(barrier, inc=1, device_id=sibling, device_id_type=MESH)
-    for p in range(1, chips):
-        pl.semaphore_signal(barrier, inc=1, device_id=peer(p), device_id_type=MESH)
-    for s in range(1, groups):
-        pl.semaphore_signal(
-            barrier, inc=1, device_id={"fsdp": lax.rem(group + s, groups)}, device_id_type=MESH
-        )
+    lead = core == 0
+    mates = [{"fsdp": lax.rem(group + s, groups)} for s in range(1, groups)]
+
+    @pl.when(lead)
+    def _():
+        for p in range(chips):
+            pl.semaphore_signal(
+                barrier, inc=1, device_id={"island": owner(p) * CORES + 1}, device_id_type=MESH
+            )
+        for mate in mates:
+            pl.semaphore_signal(barrier, inc=1, device_id=mate, device_id_type=MESH)
+
+    @pl.when(jnp.logical_not(lead))
+    def _():
+        for p in range(1, chips):
+            pl.semaphore_signal(barrier, inc=1, device_id=peer(p), device_id_type=MESH)
 
     def load(side, p):
         which = other if side == 0 else core
@@ -122,7 +132,15 @@
         mine = local[pl.ds(start_of(core, p, j), chunk)].astype(jnp.float32)
         return mine + paired[p, span(j)]
 
-    pl.semaphore_wait(barrier, 1 + (chips - 1) + (groups - 1))
+    @pl.when(jnp.logical_not(lead))
+    def _():
+        pl.semaphore_wait(barrier, chips + (chips - 1))
+        pl.semaphore_signal(ready, inc=1, device_id=sibling, device_id_type=MESH)
+
+    @pl.when(lead)
+    def _():
+        pl.semaphore_wait(ready, 1)
+
     for p in range(1, chips):
         send_pair(p)
     for p in range(1, chips):
@@ -155,40 +173,57 @@
 
     partial = lax.fori_loop(0, count, finish, jnp.zeros((8, 128), jnp.float32))
 
-    def send_sum(slots, mine, value, targets, first):
+    def sum_copy(slots, mine, number, target):
+        return pltpu.make_async_remote_copy(
+            slots.at[mine], slots.at[mine],
+            sum_send.at[number], sum_recv.at[number], target, MESH,
+        )
+
+    def send_sums(slots, mine, value, targets, first):
         slots[mine] = value
-        copies = []
-        for s, target in enumerate(targets):
-            copy = pltpu.make_async_remote_copy(
-                slots.at[mine], slots.at[mine],
-                sum_send.at[first + s], sum_recv.at[first + s], target, MESH,
-            )
+        copies = [sum_copy(slots, mine, first + s, t) for s, t in enumerate(targets)]
+        for copy in copies:
             copy.start()
-            copies.append(copy)
         return copies
 
-    def take_sum(slots, copies):
-        for copy in copies:
-            copy.wait_recv()
+    def add_up(slots):
         total = slots[0]
         for s in range(1, slots.shape[0]):
             total = total + slots[s]
         return total
 
-    sent_a = send_sum(chip_sums, chip, partial, [peer(p) for p in range(1, chips)], 1)
+    sent = send_sums(chip_sums, chip, partial, [peer(p) for p in range(1, chips)], 2)
 
     def gather_rest(j, _):
         gather(j)
 
     lax.fori_loop(min(AHEAD, count), count, gather_rest, None)
-    total = take_sum(chip_sums, sent_a)
-    sent_b = send_sum(pair_sums, core, total, [sibling], 0)
-    total = take_sum(pair_sums, sent_b)
-    sent_c = send_sum(
-        group_sums, group, total,
-        [{"fsdp": lax.rem(group + s, groups)} for s in range(1, groups)], chips,
-    )
-    squares = jnp.sum(take_sum(group_sums, sent_c), keepdims=True)
+    for copy in sent:
+        copy.wait_recv()
+    pair_sums[core] = add_up(chip_sums)
+    from_pair = sum_copy(pair_sums, 1, 0, sibling)
+    whole = sum_copy(total_sum, 0, 1, sibling)
+
+    @pl.when(jnp.logical_not(lead))
+    def _():
+        from_pair.start()
+        whole.wait_recv()
+        from_pair.wait_send()
+
+    @pl.when(lead)
+    def _():
+        pl.semaphore_wait(barrier, groups - 1)
+        from_pair.wait_recv()
+        copies = send_sums(group_sums, group, add_up(pair_sums), mates, 1 + chips)
+        for copy in copies:
+            copy.wait_recv()
+        total_sum[0] = add_up(group_sums)
+        whole.start()
+        for copy in copies:
+            copy.wait_send()
+        whole.wait_send()
+
+    squares = jnp.sum(total_sum[0], keepdims=True)
     factor = jnp.minimum(1.0, threshold / jnp.sqrt(squares + 1e-06))
     for copy in state:
         copy.wait()
@@ -232,7 +267,7 @@
             full_to_peer(p, j, 0, p).wait_send()
 
     each(close)
-    for copy in sent_a + sent_b + sent_c:
+    for copy in sent:
         copy.wait_send()
 
 
@@ -260,6 +295,7 @@
             pltpu.VMEM((CORES, 8, 128), wide),
             pltpu.VMEM((chips, 8, 128), wide),
             pltpu.VMEM((groups, 8, 128), wide),
+            pltpu.VMEM((1, 8, 128), wide),
             dma((2, chips)),
             dma((2,)),
             dma((chips, count)),
@@ -270,8 +306,9 @@
             dma((chips - 1, count)),
             dma((chips, count)),
             dma((chips, count)),
-            dma((chips + groups - 1,)),
-            dma((chips + groups - 1,)),
+            dma((chips + groups,)),
+            dma((chips + groups,)),
+            pltpu.SemaphoreType.REGULAR,
         ],
         compiler_params=pltpu.CompilerParams(
             collective_id=0, has_side_effects=True, vmem_limit_bytes=32 * 2**20
@@ -282,9 +319,33 @@
     )(*(pltpu.with_memory_space_constraint(x, pltpu.HBM) for x in (grads, outer, moment)))
 
 
+def store_kernel(params, moment, params_out, moment_out, sem):
+    part = params.shape[0] // STORES
+    copies = []
+    for s in range(STORES):
+        place = pl.ds(s * part, part)
+        for a, (source, target) in enumerate([(params, params_out), (moment, moment_out)]):
+            copies.append(pltpu.make_async_copy(source.at[place], target.at[place], sem.at[a, s]))
+    for copy in copies:
+        copy.start()
+    for copy in copies:
+        copy.wait()
+
+
+def store(results):
+    return pl.pallas_call(
+        store_kernel,
+        out_shape=[jax.ShapeDtypeStruct(x.shape, x.dtype) for x in results],
+        in_specs=[pl.BlockSpec(memory_space=pltpu.VMEM)] * 2,
+        out_specs=[pl.BlockSpec(memory_space=pltpu.HBM)] * 2,
+        scratch_shapes=[pltpu.SemaphoreType.DMA((2, STORES))],
+        compiler_params=pltpu.CompilerParams(vmem_limit_bytes=4 * 2**20),
+    )(*(pltpu.with_memory_space_constraint(x, pltpu.VMEM) for x in results))
+
+
 def per_device(pseudo_grads, outer_params, momentum):
     islands, groups = lax.axis_size("island"), lax.axis_size("fsdp")
-    return tuple(step(islands, groups, pseudo_grads, outer_params, momentum))
+    return tuple(store(step(islands, groups, pseudo_grads, outer_params, momentum)))
 
 
 def solution(mesh):

time: 61.2 us -> 57.6 us (0.941)
  local copies, waits for them, and re-layouts: 4.03 us -> 0 us
    unnamed x2 -> x0, local copies, waits for them, and re-layouts: 4.03 us -> none
    pallas_call x0 -> x1, Pallas kernels: none -> 3.37 us  [store(): pl.pallas_call(store_kernel, out_shape=[jax.ShapeDtypeStruct(x.shape, x.d...]
    pallas_call x1, Pallas kernels: 56.4 us -> 53.4 us  [step(): pl.pallas_call(functools.partial(kernel, chips, groups, chunk, threshold)...]
where the time goes in v3:
time: 57.6 us; the launch traced here: 57.4 us
  Pallas kernels  56.8 us (99%)
  between operations  0.64 us (1%)
    pallas_call x1, Pallas kernels, step(): pl.pallas_call(functools.partial(kernel, chips, groups, chunk, threshold)...  53.4 us
    pallas_call x1, Pallas kernels, store(): pl.pallas_call(store_kernel, out_shape=[jax.ShapeDtypeStruct(x.shape, x.d...  3.37 us

profile of v3, /device:TPU:0, one launch (start us, length us, event | category | flops | bytes accessed | tf_op | source)
XLA Modules:
  0.0 57.4 jit_solution(13038434846915885121)
XLA Ops:
  0.6 53.4 %shard_map.50 = (f32[1024,1024]{1,0:T(8,128)S(1)}, f32[1024,1024]{1,0:T(8,128)S(1)}) custom-call(bf16[1,1024,1024]{2,1,0:T(8,128)(2,1)} %grads.1, f32[1024,1024]{1,0:T(8,128)} %outer.1, f32[1024,1024]{1,0:T(8,128)} %moment.1), custom_call_target="tpu_custom_call" | custom-call | flops 16777216 | bytes 10485760 | tf_op jit(solution)/shard_map/pallas_call | solution.py:283
  54.1 3.4 %shard_map.51 = (f32[1024,1024]{1,0:T(8,128)}, f32[1024,1024]{1,0:T(8,128)}) custom-call(f32[1024,1024]{1,0:T(8,128)S(1)} %get-tuple-element.4.params, f32[1024,1024]{1,0:T(8,128)S(1)} %get-tuple-element.5.moment), custom_call_target="tpu_custom_call" | custom-call | tf_op jit(solution)/shard_map/pallas_call | solution.py:336

commit v4 on v3

--- a/solution.py
+++ b/solution.py
@@ -10,7 +10,7 @@
 
 MESH = pl.DeviceIdType.MESH
 CORES = 2
-CHUNKS = 8
+CHUNKS = 4
 AHEAD = 2
 STORES = 4
 
@@ -117,21 +117,18 @@
     def each(body):
         lax.fori_loop(0, count, lambda j, _: body(j), None)
 
-    def send_pair(p):
-        load(0, p).wait()
-
-        def body(j):
-            block = local[pl.ds(start_of(other, p, j), chunk)]
-            staged[p, span(j)] = block.astype(jnp.float32)
-            to_sibling(p, j).start()
-
-        each(body)
+    def stage(p, j):
+        block = local[pl.ds(start_of(other, p, j), chunk)]
+        staged[p, span(j)] = block.astype(jnp.float32)
 
     def chip_sum(p, j):
         to_sibling(p, j).wait_recv()
         mine = local[pl.ds(start_of(core, p, j), chunk)].astype(jnp.float32)
         return mine + paired[p, span(j)]
 
+    for p in range(1, chips):
+        load(0, p).wait()
+        each(lambda j, p=p: stage(p, j))
     @pl.when(jnp.logical_not(lead))
     def _():
         pl.semaphore_wait(barrier, chips + (chips - 1))
@@ -142,7 +139,7 @@
         pl.semaphore_wait(ready, 1)
 
     for p in range(1, chips):
-        send_pair(p)
+        each(lambda j, p=p: to_sibling(p, j).start())
     for p in range(1, chips):
         load(1, p).wait()
 
@@ -151,6 +148,12 @@
             part_to_peer(p, j, True).start()
 
         each(send_part)
+    load(0, 0).wait()
+
+    def send_pair(j):
+        stage(0, j)
+        to_sibling(0, j).start()
+
     send_pair(0)
     load(1, 0).wait()
     for copy in state:
@@ -161,6 +164,7 @@
             full_to_peer(p, j, 0, chips - p).start()
 
     def finish(j, partial):
+        pl.when(j + 1 < count)(lambda: send_pair(j + 1))
         total = chip_sum(0, j)
         for p in range(1, chips):
             part_to_peer(p, j, False).wait_recv()

time: 57.6 us -> 57.6 us (level)
  no operation moved by 1% of the time
where the time goes in v4:
time: 57.6 us; the launch traced here: 57.5 us
  Pallas kernels  56.9 us (99%)
  between operations  0.64 us (1%)
    pallas_call x1, Pallas kernels, step(): pl.pallas_call(functools.partial(kernel, chips, groups, chunk, threshold)...  53.5 us
    pallas_call x1, Pallas kernels, store(): pl.pallas_call(store_kernel, out_shape=[jax.ShapeDtypeStruct(x.shape, x.d...  3.37 us

profile of v4, /device:TPU:0, one launch (start us, length us, event | category | flops | bytes accessed | tf_op | source)
XLA Modules:
  0.0 57.5 jit_solution(16013231896377678888)
XLA Ops:
  0.6 53.5 %shard_map.50 = (f32[1024,1024]{1,0:T(8,128)S(1)}, f32[1024,1024]{1,0:T(8,128)S(1)}) custom-call(bf16[1,1024,1024]{2,1,0:T(8,128)(2,1)} %grads.1, f32[1024,1024]{1,0:T(8,128)} %outer.1, f32[1024,1024]{1,0:T(8,128)} %moment.1), custom_call_target="tpu_custom_call" | custom-call | flops 16777216 | bytes 10485760 | tf_op jit(solution)/shard_map/pallas_call | solution.py:287
  54.1 3.4 %shard_map.51 = (f32[1024,1024]{1,0:T(8,128)}, f32[1024,1024]{1,0:T(8,128)}) custom-call(f32[1024,1024]{1,0:T(8,128)S(1)} %get-tuple-element.4.params, f32[1024,1024]{1,0:T(8,128)S(1)} %get-tuple-element.5.moment), custom_call_target="tpu_custom_call" | custom-call | tf_op jit(solution)/shard_map/pallas_call | solution.py:340
